TPU v7x, 32 devices: a whole 2x2x4 slice. The times are simulated.
32 devices in a mesh: ta: 4 (over z), ha: 2 (over y), wa: 4 (over x, core).
Axes of the slice: x: 2, y: 2, z: 4, core: 2. Of those that a mesh axis runs over, the one named last changes fastest.
Arguments:
- stream: bfloat16 [4, 2, 384, 1536], P('ta', 'ha'), may hold values from -40 to 40
- queries: bfloat16 [4, 2, 384, 1536], P('ta', 'ha', None, 'wa'), may hold values from -6 to 6
- key_heads: bfloat16 [4, 2, 384, 1536], P('ta', 'ha', None, 'wa'), may hold values from -6 to 6
- value_heads: bfloat16 [4, 2, 384, 1536], P('ta', 'ha', None, 'wa'), may hold values from -6 to 6
- out_weight: bfloat16 [1536, 1536], P('wa'), may hold values from -0.15625 to 0.15625
- norm_gain: float32 [1536], replicated, may hold values from 0.25 to 1.75
- up_weight: bfloat16 [1536, 6144], P(('ta', 'ha'), 'wa'), may hold values from -0.15625 to 0.15625
- down_weight: bfloat16 [6144, 1536], P('wa', ('ta', 'ha')), may hold values from -0.078125 to 0.078125
- tile_route: int32 [4, 2, 1], P('ta', 'ha'), may hold values 0 or 1
- cotangent: bfloat16 [4, 2, 384, 1536], P('ta', 'ha'), may hold values from -6 to 6
Outputs:
- stream_grad: bfloat16 [4, 2, 384, 1536], P('ta', 'ha')
- query_grad: bfloat16 [4, 2, 384, 1536], P('ta', 'ha', None, 'wa')
- key_grad: bfloat16 [4, 2, 384, 1536], P('ta', 'ha', None, 'wa')
- value_grad: bfloat16 [4, 2, 384, 1536], P('ta', 'ha', None, 'wa')
- out_weight_grad: float32 [1536, 1536], P('wa', ('ta', 'ha'))
All inputs are finite; a program needn't handle non-finite values. No bound on the sum of `tile_route` on one device may be relied on, other than what follows from the above.
Results may differ from a plain program's by a relative error of at most 0.014.
Values may be sent and summed in bfloat16 or wider, within the bound.
A program may use at most 128 MiB of HBM per device.

v0:
```python
import math
import jax
import jax.numpy as jnp
from jax import lax
from jax.sharding import PartitionSpec as P

HS = 128
TILE = 384
EPSILON = 1e-06
TANH_SCALE = 0.7978845608028654
CUBIC_COEF = 0.044715
NEG_FILL = -1e30


def extended(cells, sides, width):
    for axis, dim in sides:
        count = lax.axis_size(axis)
        ends = count - 1
        head = lax.slice_in_dim(cells, 0, width, axis=dim)
        tail = lax.slice_in_dim(cells, cells.shape[dim] - width, cells.shape[dim], axis=dim)
        cells = jnp.concatenate(
            [
                lax.ppermute(tail, axis, [(i, (i + 1) % count) for i in range(ends)]),
                cells,
                lax.ppermute(head, axis, [((i + 1) % count, i) for i in range(ends)]),
            ],
            axis=dim,
        )
    return cells


def from_behind(array, axis, by):
    devices = lax.axis_size(axis)
    pairs = [(i, i + by) for i in range(devices) if 0 <= i + by < devices]
    return lax.ppermute(array, axis, pairs)


def gelu_slope(pre_act):
    tanh_arg = TANH_SCALE * (pre_act + CUBIC_COEF * pre_act * pre_act * pre_act)
    tanh_val = jnp.tanh(tanh_arg)
    return 0.5 * (1.0 + tanh_val) + 0.5 * pre_act * (1.0 - tanh_val * tanh_val) * TANH_SCALE * (
        1.0 + 3.0 * CUBIC_COEF * pre_act * pre_act
    )


def head_probs(query_rows, key_rows, key_marks, score_scale):
    scores = (
        jnp.einsum("qd,kd->qk", query_rows, key_rows, preferred_element_type=jnp.float32)
        * score_scale
    )
    scores = jnp.where(key_marks[None, :] > 0.5, scores, NEG_FILL)
    row_max = jnp.max(scores, axis=1)
    weights = jnp.exp(scores - row_max[:, None])
    row_total = jnp.sum(weights, axis=1)
    return (weights / row_total[:, None], row_max, row_total)


def layer_norm(residual):
    mean_val = jnp.mean(residual, axis=1, keepdims=True)
    centered = residual - mean_val
    variance = jnp.mean(centered * centered, axis=1, keepdims=True)
    inv_std = lax.rsqrt(variance + EPSILON)
    return (centered * inv_std, inv_std)


def norm_backward(norm_grad, norm_gain, normed, inv_std):
    scaled = norm_grad * norm_gain
    return (
        scaled
        - jnp.mean(scaled, axis=1, keepdims=True)
        - normed * jnp.mean(scaled * normed, axis=1, keepdims=True)
    ) * inv_std


def shards(
    stream,
    queries,
    key_heads,
    value_heads,
    out_weight,
    norm_gain,
    up_weight,
    down_weight,
    tile_route,
    cotangent,
):
    row_count = stream.shape[2]
    model_width = stream.shape[3]
    channels = queries.shape[3]
    heads_here = channels // HS
    tile_count = row_count // TILE
    score_scale = 1.0 / math.sqrt(HS)
    tile_ids = jnp.arange(tile_count, dtype=jnp.int32)
    tile_marks = tile_route.astype(jnp.bfloat16)
    faces_key, faces_value, faces_marks = (
        extended(key_heads, (("ta", 0), ("ha", 1)), 1),
        extended(value_heads, (("ta", 0), ("ha", 1)), 1),
        extended(tile_marks, (("ta", 0), ("ha", 1)), 1),
    )

    def window():
        key_block = faces_key.reshape(9 * TILE, heads_here, HS)
        value_block = faces_value.reshape(9 * TILE, heads_here, HS)
        mark_block = faces_marks.reshape(9).astype(jnp.float32)
        key_marks = jnp.repeat(mark_block, TILE)
        query_tile = queries.reshape(TILE, heads_here, HS)
        return (
            query_tile.transpose(1, 0, 2),
            key_block.transpose(1, 0, 2),
            value_block.transpose(1, 0, 2),
            key_marks,
        )

    def forward_tile(tile_index):
        own_mark = tile_marks[0, 0, tile_index]
        query_tile, key_block, value_block, key_marks = window()

        def per_head(operands):
            query_rows, key_rows, value_rows = operands
            weights, row_max, row_total = head_probs(query_rows, key_rows, key_marks, score_scale)
            mixture = jnp.dot(
                weights.astype(jnp.bfloat16), value_rows, preferred_element_type=jnp.float32
            )
            return (mixture, row_max, row_total)

        mixture, row_max, row_total = lax.map(per_head, (query_tile, key_block, value_block))
        scaled = (mixture * own_mark.astype(jnp.float32)).astype(jnp.bfloat16)
        return (scaled.transpose(1, 0, 2).reshape(TILE, channels), row_max, row_total)

    attn_tiles, max_tiles, total_tiles = lax.map(forward_tile, tile_ids)
    attention = attn_tiles.reshape(row_count, channels)
    attn_part = jnp.dot(attention, out_weight, preferred_element_type=jnp.float32)
    head_share = lax.psum_scatter(attn_part, "wa", scatter_dimension=0, tiled=True)
    share_rows = head_share.shape[0]
    share_start = lax.axis_index("wa") * share_rows
    flat_stream = stream.reshape(row_count, model_width)
    flat_cot = cotangent.reshape(row_count, model_width)
    residual = (
        lax.dynamic_slice_in_dim(flat_stream, share_start, share_rows, 0).astype(jnp.float32)
        + head_share
    )
    normed, inv_std = layer_norm(residual)
    hidden_share = (normed * norm_gain).astype(jnp.bfloat16)
    hidden_in = lax.all_gather(hidden_share, "wa", axis=0, tiled=True)
    up_full, down_full = (
        lax.all_gather(up_weight, ("ta", "ha"), axis=0, tiled=True),
        lax.all_gather(down_weight, ("ta", "ha"), axis=1, tiled=True),
    )
    pre_act = jnp.dot(hidden_in, up_full, preferred_element_type=jnp.float32)
    act_grad = jnp.einsum("td,fd->tf", flat_cot, down_full, preferred_element_type=jnp.float32)
    pre_grad = (act_grad * gelu_slope(pre_act)).astype(jnp.bfloat16)
    norm_part = jnp.einsum("tf,df->td", pre_grad, up_full, preferred_element_type=jnp.float32)
    norm_share = lax.psum_scatter(norm_part, "wa", scatter_dimension=0, tiled=True)
    cot_share = lax.dynamic_slice_in_dim(flat_cot, share_start, share_rows, 0).astype(jnp.float32)
    grad_share = (cot_share + norm_backward(norm_share, norm_gain, normed, inv_std)).astype(
        jnp.bfloat16
    )
    stream_grad = lax.all_gather(grad_share, "wa", axis=0, tiled=True)
    weight_part = jnp.einsum(
        "tc,td->cd", attention, stream_grad, preferred_element_type=jnp.float32
    )
    out_weight_grad = lax.psum_scatter(weight_part, ("ta", "ha"), scatter_dimension=1, tiled=True)
    attn_grad = jnp.einsum(
        "td,cd->tc", stream_grad, out_weight, preferred_element_type=jnp.float32
    ).astype(jnp.bfloat16)
    row_marks = jnp.repeat(tile_marks.reshape(tile_count), TILE)
    masked_grad = attn_grad * row_marks[:, None]

    def own_side():
        query_tile, key_block, value_block, key_marks = window()
        grad_tile = masked_grad.reshape(TILE, heads_here, HS).transpose(1, 0, 2)

        def head_back(operands):
            query_rows, key_rows, value_rows, grad_rows = operands
            weights = head_probs(query_rows, key_rows, key_marks, score_scale)[0]
            grad_probs = jnp.einsum(
                "qd,kd->qk", grad_rows, value_rows, preferred_element_type=jnp.float32
            )
            row_delta = jnp.sum(weights * grad_probs, axis=1)
            grad_scores = (weights * (grad_probs - row_delta[:, None]) * score_scale).astype(
                jnp.bfloat16
            )
            query_part = jnp.dot(grad_scores, key_rows, preferred_element_type=jnp.float32).astype(
                jnp.bfloat16
            )
            value_part = jnp.einsum(
                "qk,qd->kd",
                weights.astype(jnp.bfloat16),
                grad_rows,
                preferred_element_type=jnp.float32,
            ).astype(jnp.bfloat16)
            key_part = jnp.einsum(
                "qk,qd->kd", grad_scores, query_rows, preferred_element_type=jnp.float32
            ).astype(jnp.bfloat16)
            return (query_part, row_delta, key_part, value_part)

        results = lax.map(head_back, (query_tile, key_block, value_block, grad_tile))
        query_part = results[0].transpose(1, 0, 2).reshape(TILE, channels)
        key_part = results[2].transpose(1, 0, 2).reshape(3, 3, TILE, channels)
        value_part = results[3].transpose(1, 0, 2).reshape(3, 3, TILE, channels)
        return (query_part, results[1], key_part, value_part)

    def guarded_own():
        blank_parts = (
            jnp.zeros((TILE, channels), jnp.bfloat16),
            jnp.zeros((heads_here, TILE), jnp.float32),
        )
        blank_parts = blank_parts + (
            jnp.zeros((3, 3, TILE, channels), jnp.bfloat16),
            jnp.zeros((3, 3, TILE, channels), jnp.bfloat16),
        )
        return own_side()

    def place_tile(carried, tile_index):
        query_part, row_delta, key_part, value_part = guarded_own()
        return ((key_part, value_part), query_part)

    empty_slots = jnp.zeros((3, 3, row_count, channels), jnp.bfloat16)
    (slots_key, slots_value), query_parts = lax.scan(
        place_tile, (empty_slots, empty_slots), tile_ids
    )
    middle_key = slots_key[1].astype(jnp.float32)
    middle_value = slots_value[1].astype(jnp.float32)
    for by_step, source in ((-1, 0), (1, 2)):
        moved_key, moved_value = from_behind(
            (slots_key[source], slots_value[source]), "ta", by_step
        )
        middle_key = middle_key + moved_key.astype(jnp.float32)
        middle_value = middle_value + moved_value.astype(jnp.float32)
    final_key = middle_key[1]
    final_value = middle_value[1]
    for by_step, source in ((-1, 0), (1, 2)):
        moved_key, moved_value = (
            from_behind(middle_key[source].astype(jnp.bfloat16), "ha", by_step).astype(jnp.float32),
            from_behind(middle_value[source].astype(jnp.bfloat16), "ha", by_step).astype(
                jnp.float32
            ),
        )
        final_key = final_key + moved_key
        final_value = final_value + moved_value
    key_grad = final_key.astype(jnp.bfloat16).reshape(1, 1, row_count, channels)
    value_grad = final_value.astype(jnp.bfloat16).reshape(1, 1, row_count, channels)
    query_grad = query_parts.reshape(1, 1, row_count, channels)
    return (
        stream_grad.reshape(1, 1, row_count, model_width),
        query_grad,
        key_grad,
        value_grad,
        out_weight_grad,
    )


def solution(mesh):
    placed = (
        P("ta", "ha", None, None),
        P("ta", "ha", None, "wa"),
        P("ta", "ha", None, "wa"),
        P("ta", "ha", None, "wa"),
        P("wa", None),
        P(),
        P(("ta", "ha"), "wa"),
        P("wa", ("ta", "ha")),
        P("ta", "ha", None),
        P("ta", "ha", None, None),
    )
    return jax.shard_map(
        shards,
        mesh=mesh,
        in_specs=placed,
        out_specs=(
            P("ta", "ha", None, None),
            P("ta", "ha", None, "wa"),
            P("ta", "ha", None, "wa"),
            P("ta", "ha", None, "wa"),
            P("wa", ("ta", "ha")),
        ),
        check_vma=False,
    )
```

profile of v0, /device:TPU:0, one launch (start us, length us, event | category | flops | bytes accessed | tf_op | source)
XLA Modules:
  0.0 548.8 jit_solution(6073854629250690570)
XLA Ops:
  30.7 6.4 %collective-permute-start.6 = (bf16[3,1,384,384]{3,2,1,0:T(8,128)(2,1)S(1)}, bf16[3,1,384,384]{3,2,1,0:T(8,128)(2,1)}, u32[]{:S(2)}, u32[]{:S(2)}) collective-permute-start(bf16[3,1,384,384]{3,2,1,0:T(8,128)(2,1)S(1)} %constant_dynamic-update-slice_fusion.1), channel_id=1, source_target_pairs={{0,4},{1,5},{2,6},{3,7},{8,12},{9,13},{10,14},{11,15},{16,20},{17,... | collective-permute-start | bytes 2654216 | tf_op jit(solution)/shard_map/ppermute | solution.py:23
  51.0 5.5 collective-permute-start.2
  56.6 6.5 %collective-permute-done.2 = bf16[3,1,1]{0,2,1:T(2,128)(2,1)S(1)} collective-permute-done((bf16[3,1,1]{0,2,1:T(2,128)(2,1)S(1)}, bf16[3,1,1]{0,2,1:T(2,128)(2,1)S(1)}, u32[]{:S(2)}, u32[]{:S(2)}) %collective-permute-start.2) | collective-permute-done | bytes 38 | tf_op jit(solution)/shard_map/ppermute | solution.py:23
  72.1 7.7 %reshape.147 = bf16[3456,3,128]{2,1,0:T(4,128)(2,1)} reshape(bf16[3,3,384,384]{3,2,1,0:T(8,128)(2,1)} %pad_maximum_fusion.1) | data formatting | bytes 5308416 | tf_op jit(solution)/shard_map/while/body/eval_jaxpr/reshape | solution.py:103
  87.0 7.7 %reshape.146 = bf16[3456,3,128]{2,1,0:T(4,128)(2,1)} reshape(bf16[3,3,384,384]{3,2,1,0:T(8,128)(2,1)} %pad_maximum_fusion) | data formatting | bytes 5308416 | tf_op jit(solution)/shard_map/while/body/eval_jaxpr/reshape | solution.py:102
  98.7 16.9 %while.44 = (s32[]{:T(128)}, f32[3,384,128]{1,2,0:T(8,128)S(1)}, bf16[3,384,128]{2,1,0:T(8,128)(2,1)S(1)}, bf16[3,3456,128]{2,1,0:T(8,128)(2,1)}, bf16[3,3456,128]{2,1,0:T(8,128)(2,1)}, /*index=5*/f32[9]{0:T(128)S(1)}, s32[]{:T(128)}) while((s32[]{:T(128)}, f32[3,384,128]{1,2,0:T(8,128)S(1)}, bf16[3,384,128]{2,1,0:T(8,128)(2,1)S(1)}, ...), condition=%wide.region_3.4_spmd.clone, body=%wide.region_0.3_spmd.clone.sunk | while | flops 690093312 | bytes 18014980 | solution.py:126
  118.0 32.4 %reduce-scatter.4.cloned.1.call-done = f32[96,1536]{1,0:T(8,128)} async-done(((f32[384,1536]{1,0:T(8,128)}), f32[96,1536]{1,0:T(8,128)}) %reduce-scatter.4.cloned.1.call-update) | async-done | bytes 589840 | tf_op jit(solution)/shard_map/reduce_scatter | solution.py:133
  154.7 15.8 %all-gather.7.cloned.1.call-done = bf16[384,1536]{1,0:T(8,128)(2,1)} async-done(((bf16[96,1536]{1,0:T(8,128)(2,1)}), bf16[384,1536]{1,0:T(8,128)(2,1)}) %all-gather.7.cloned.1.call-update) | async-done | bytes 1179664 | tf_op jit(solution)/shard_map/all_gather | solution.py:144
  170.5 82.3 %all-gather.9.cloned.1.call-done = bf16[1536,1536]{1,0:T(8,128)(2,1)} async-done(((bf16[192,1536]{1,0:T(8,128)(2,1)}), bf16[1536,1536]{1,0:T(8,128)(2,1)}) %all-gather.9.cloned.1.call-update) | async-done | bytes 4718608 | tf_op jit(solution)/shard_map/all_gather | solution.py:146
  252.8 6.1 %fusion.80 = f32[384,1536]{1,0:T(8,128)} fusion(bf16[384,1536]{1,0:T(8,128)(2,1)} %all-gather.7.cloned.1.call-done, bf16[1536,1536]{1,0:T(8,128)(2,1)} %all-gather.9.cloned.1.call-done), kind=kOutput, calls=%fused_computation.124 | convolution fusion | flops 1811939328 | bytes 8257536 | tf_op jit(solution)/shard_map/dot_general | solution.py:149
  258.9 74.3 %all-gather.5.cloned.1.call-done = bf16[1536,1536]{0,1:T(8,128)(2,1)} async-done(((bf16[1536,192]{0,1:T(8,128)(2,1)}), bf16[1536,1536]{0,1:T(8,128)(2,1)}) %all-gather.5.cloned.1.call-update) | async-done | bytes 4718608 | tf_op jit(solution)/shard_map/all_gather | solution.py:147
  333.1 10.0 %fusion.56 = f32[384,1536]{1,0:T(8,128)} fusion(bf16[1536,1536]{1,0:T(8,128)(2,1)} %all-gather.9.cloned.1.call-done, bf16[1536,1536]{0,1:T(8,128)(2,1)} %all-gather.5.cloned.1.call-done, f32[384,1536]{1,0:T(8,128)} %fusion.80, bf16[1,1,384,1536]{3,2,1,0:T(8,128)(2,1)} %param.23), kind=kOutput, calls=%fused_computation.75 | convolution fusion | flops 3635085312 | bytes 15335424 | tf_op jit(solution)/shard_map/tf,df->td/dot_general | solution.py:152
  343.3 31.3 %reduce-scatter.6.cloned.1.call-done = f32[96,1536]{1,0:T(8,128)} async-done(((f32[384,1536]{1,0:T(8,128)}), f32[96,1536]{1,0:T(8,128)}) %reduce-scatter.6.cloned.1.call-update) | async-done | bytes 589840 | tf_op jit(solution)/shard_map/reduce_scatter | solution.py:153
  378.2 17.5 %all-gather.11.cloned.1.call-done = bf16[384,1536]{1,0:T(8,128)(2,1)} async-done(((bf16[96,1536]{1,0:T(8,128)(2,1)}), bf16[384,1536]{1,0:T(8,128)(2,1)}) %all-gather.11.cloned.1.call-update) | async-done | bytes 1179664 | tf_op jit(solution)/shard_map/all_gather | solution.py:158
  400.5 43.7 %while.45 = (s32[]{:T(128)}, bf16[3,384,128]{1,2,0:T(8,128)(2,1)S(1)}, bf16[3,3456,128]{2,1,0:T(8,128)(2,1)}, bf16[3,3456,128]{2,1,0:T(8,128)(2,1)}, bf16[3,384,...) while((s32[]{:T(128)}, ...), condition=%wide.region_14.15_spmd.clone, body=%wide.region_10.14_spmd.clone.sunk | while | flops 1723513728 | bytes 71701848 | solution.py:197
  447.1 5.5 copy.58
  456.0 5.6 %copy.59 = bf16[1152,3,128]{2,1,0:T(4,128)(2,1)S(1)} copy(bf16[1152,3,128]{2,0,1:T(8,128)(2,1)} %get-tuple-element.257) | data formatting | bytes 1769472 | tf_op jit(solution)/shard_map/slice | solution.py:226
  463.6 5.5 collective-permute-start.17
  472.5 5.5 copy.55
  481.3 5.6 %copy.56 = bf16[1152,3,128]{2,1,0:T(4,128)(2,1)S(1)} copy(bf16[1152,3,128]{2,0,1:T(8,128)(2,1)} %get-tuple-element.260) | data formatting | bytes 1769472 | tf_op jit(solution)/shard_map/slice | solution.py:226
  488.9 5.7 %collective-permute-start.13 = (bf16[3,384,384]{2,1,0:T(8,128)(2,1)}, bf16[3,384,384]{2,1,0:T(8,128)(2,1)}, u32[]{:S(2)}, u32[]{:S(2)}) collective-permute-start(bf16[3,384,384]{2,1,0:T(8,128)(2,1)} %squeeze.56), channel_id=1, source_target_pairs={{0,8},{8,16},{16,24},{1,9},{9,17},{17,25},{2,10},{10,18},{18,26},{... | collective-permute-start | bytes 2654216 | tf_op jit(solution)/shard_map/ppermute | solution.py:35
  494.6 5.9 %copy.57 = f32[1152,3,128]{2,1,0:T(4,128)} copy(f32[1152,3,128]{2,0,1:T(8,128)S(1)} %get-tuple-element.258) | data formatting | bytes 3538944 | tf_op jit(solution)/shard_map/convert_element_type | solution.py:223
  504.8 5.9 %copy.54 = f32[1152,3,128]{2,1,0:T(4,128)} copy(f32[1152,3,128]{2,0,1:T(8,128)S(1)} %copy-done.2) | data formatting | bytes 3538944 | tf_op jit(solution)/shard_map/convert_element_type | solution.py:222
  529.5 5.3 collective-permute-start.15
  (182 shorter events, 179.1 us)
Async XLA Ops:
  7.2 143.2 %reduce-scatter.4.cloned.1.call-start = ((), (), s32[]{:S(2)}) async-start(), calls=%async_computation.4 | async-start | bytes 2949120 | tf_op jit(solution)/shard_map/reduce_scatter | solution.py:133
  7.2 12.6 %collective-permute-start.8 = (bf16[1,1,384,384]{3,2,1,0:T(8,128)(2,1)}, bf16[1,1,384,384]{3,2,1,0:T(8,128)(2,1)S(1)}, u32[]{:S(2)}, u32[]{:S(2)}) collective-permute-start(bf16[1,1,384,384]{3,2,1,0:T(8,128)(2,1)} %param.17), channel_id=1, source_target_pairs={{0,8},{8,16},{16,24},{1,9},{9,17},{17,25},{2,10},{10,18},{18,26},{... | collective-permute-start | bytes 884744 | tf_op jit(solution)/shard_map/ppermute | solution.py:23
  12.3 11.5 %collective-permute-start.9 = (bf16[1,1,384,384]{3,2,1,0:T(8,128)(2,1)}, bf16[1,1,384,384]{3,2,1,0:T(8,128)(2,1)S(1)}, u32[]{:S(2)}, u32[]{:S(2)}) collective-permute-start(bf16[1,1,384,384]{3,2,1,0:T(8,128)(2,1)} %param.17), channel_id=1, source_target_pairs={{8,0},{16,8},{24,16},{9,1},{17,9},{25,17},{10,2},{18,10},{26,18},{... | collective-permute-start | bytes 884744 | tf_op jit(solution)/shard_map/ppermute | solution.py:25
  13.6 15.9 %collective-permute-start.4 = (bf16[1,1,384,384]{3,2,1,0:T(8,128)(2,1)}, bf16[1,1,384,384]{3,2,1,0:T(8,128)(2,1)S(1)}, u32[]{:S(2)}, u32[]{:S(2)}) collective-permute-start(bf16[1,1,384,384]{3,2,1,0:T(8,128)(2,1)} %param.16), channel_id=1, source_target_pairs={{0,8},{8,16},{16,24},{1,9},{9,17},{17,25},{2,10},{10,18},{18,26},{... | collective-permute-start | bytes 884744 | tf_op jit(solution)/shard_map/ppermute | solution.py:23
  18.2 12.4 %collective-permute-start.5 = (bf16[1,1,384,384]{3,2,1,0:T(8,128)(2,1)}, bf16[1,1,384,384]{3,2,1,0:T(8,128)(2,1)S(1)}, u32[]{:S(2)}, u32[]{:S(2)}) collective-permute-start(bf16[1,1,384,384]{3,2,1,0:T(8,128)(2,1)} %param.16), channel_id=1, source_target_pairs={{8,0},{16,8},{24,16},{9,1},{17,9},{25,17},{10,2},{18,10},{26,18},{... | collective-permute-start | bytes 884744 | tf_op jit(solution)/shard_map/ppermute | solution.py:25
  23.9 44.9 %collective-permute-start.10 = (bf16[3,1,384,384]{3,2,1,0:T(8,128)(2,1)S(1)}, bf16[3,1,384,384]{3,2,1,0:T(8,128)(2,1)}, u32[]{:S(2)}, u32[]{:S(2)}) collective-permute-start(bf16[3,1,384,384]{3,2,1,0:T(8,128)(2,1)S(1)} %constant_dynamic-update-slice_fusion.4), channel_id=1, source_target_pairs={{0,4},{1,5},{2,6},{3,7},{8,12},{9,13},{10,14},{11,15},{16,20},{17,... | collective-permute-start | bytes 2654216 | tf_op jit(solution)/shard_map/ppermute | solution.py:23
  28.3 40.5 %collective-permute-start.11 = (bf16[3,1,384,384]{3,2,1,0:T(8,128)(2,1)S(1)}, bf16[3,1,384,384]{3,2,1,0:T(8,128)(2,1)}, u32[]{:S(2)}, u32[]{:S(2)}) collective-permute-start(bf16[3,1,384,384]{3,2,1,0:T(8,128)(2,1)S(1)} %constant_dynamic-update-slice_fusion.4), channel_id=1, source_target_pairs={{4,0},{5,1},{6,2},{7,3},{12,8},{13,9},{14,10},{15,11},{20,16},{21,... | collective-permute-start | bytes 2654216 | tf_op jit(solution)/shard_map/ppermute | solution.py:25
  30.7 53.0 %collective-permute-start.6 = (bf16[3,1,384,384]{3,2,1,0:T(8,128)(2,1)S(1)}, bf16[3,1,384,384]{3,2,1,0:T(8,128)(2,1)}, u32[]{:S(2)}, u32[]{:S(2)}) collective-permute-start(bf16[3,1,384,384]{3,2,1,0:T(8,128)(2,1)S(1)} %constant_dynamic-update-slice_fusion.1), channel_id=1, source_target_pairs={{0,4},{1,5},{2,6},{3,7},{8,12},{9,13},{10,14},{11,15},{16,20},{17,... | collective-permute-start | bytes 2654216 | tf_op jit(solution)/shard_map/ppermute | solution.py:23
  37.1 46.6 %collective-permute-start.7 = (bf16[3,1,384,384]{3,2,1,0:T(8,128)(2,1)S(1)}, bf16[3,1,384,384]{3,2,1,0:T(8,128)(2,1)}, u32[]{:S(2)}, u32[]{:S(2)}) collective-permute-start(bf16[3,1,384,384]{3,2,1,0:T(8,128)(2,1)S(1)} %constant_dynamic-update-slice_fusion.1), channel_id=1, source_target_pairs={{4,0},{5,1},{6,2},{7,3},{12,8},{13,9},{14,10},{15,11},{20,16},{21,... | collective-permute-start | bytes 2654216 | tf_op jit(solution)/shard_map/ppermute | solution.py:25
  51.0 12.1 %collective-permute-start.2 = (bf16[3,1,1]{0,2,1:T(2,128)(2,1)S(1)}, bf16[3,1,1]{0,2,1:T(2,128)(2,1)S(1)}, u32[]{:S(2)}, u32[]{:S(2)}) collective-permute-start(bf16[3,1,1]{0,2,1:T(2,128)(2,1)S(1)} %pad_maximum_fusion.2), channel_id=1, source_target_pairs={{0,4},{1,5},{2,6},{3,7},{8,12},{9,13},{10,14},{11,15},{16,20},{17,... | collective-permute-start | bytes 26 | tf_op jit(solution)/shard_map/ppermute | solution.py:23
  117.9 52.5 %all-gather.7.cloned.1.call-start = ((), (), s32[]{:S(2)}) async-start(), calls=%async_computation.5 | async-start | bytes 1474560 | tf_op jit(solution)/shard_map/all_gather | solution.py:144
  152.8 100.0 %all-gather.9.cloned.1.call-start = ((), (), s32[]{:S(2)}) async-start(), calls=%async_computation.6 | async-start | bytes 5308416 | tf_op jit(solution)/shard_map/all_gather | solution.py:146
  153.6 179.6 %all-gather.5.cloned.1.call-start = ((), (), s32[]{:S(2)}) async-start(), calls=%async_computation.3 | async-start | bytes 5308416 | tf_op jit(solution)/shard_map/all_gather | solution.py:147
  154.2 220.4 %reduce-scatter.6.cloned.1.call-start = ((), (), s32[]{:S(2)}) async-start(), calls=%async_computation.7 | async-start | bytes 2949120 | tf_op jit(solution)/shard_map/reduce_scatter | solution.py:153
  343.2 52.6 %all-gather.11.cloned.1.call-start = ((), (), s32[]{:S(2)}) async-start(), calls=%async_computation.8 | async-start | bytes 1474560 | tf_op jit(solution)/shard_map/all_gather | solution.py:158
  378.1 162.6 %reduce-scatter.8.cloned.1.call-start = ((), (), s32[]{:S(2)}) async-start(), calls=%async_computation.9 | async-start | bytes 2654208 | tf_op jit(solution)/shard_map/reduce_scatter | solution.py:162
  454.6 59.0 %collective-permute-start.16 = (bf16[3,384,384]{2,1,0:T(8,128)(2,1)}, bf16[3,384,384]{2,1,0:T(8,128)(2,1)}, u32[]{:S(2)}, u32[]{:S(2)}) collective-permute-start(bf16[3,384,384]{2,1,0:T(8,128)(2,1)} %squeeze.58), channel_id=1, source_target_pairs={{8,0},{16,8},{24,16},{9,1},{17,9},{25,17},{10,2},{18,10},{26,18},{... | collective-permute-start | bytes 2654216 | tf_op jit(solution)/shard_map/ppermute | solution.py:35
  463.6 50.0 %collective-permute-start.17 = (bf16[3,384,384]{2,1,0:T(8,128)(2,1)}, bf16[3,384,384]{2,1,0:T(8,128)(2,1)}, u32[]{:S(2)}, u32[]{:S(2)}) collective-permute-start(bf16[3,384,384]{2,1,0:T(8,128)(2,1)} %squeeze.59), channel_id=1, source_target_pairs={{0,8},{8,16},{16,24},{1,9},{9,17},{17,25},{2,10},{10,18},{18,26},{... | collective-permute-start | bytes 2654216 | tf_op jit(solution)/shard_map/ppermute | solution.py:35
  480.0 44.5 %collective-permute-start.12 = (bf16[3,384,384]{2,1,0:T(8,128)(2,1)}, bf16[3,384,384]{2,1,0:T(8,128)(2,1)}, u32[]{:S(2)}, u32[]{:S(2)}) collective-permute-start(bf16[3,384,384]{2,1,0:T(8,128)(2,1)} %squeeze.55), channel_id=1, source_target_pairs={{8,0},{16,8},{24,16},{9,1},{17,9},{25,17},{10,2},{18,10},{26,18},{... | collective-permute-start | bytes 2654216 | tf_op jit(solution)/shard_map/ppermute | solution.py:35
  488.9 35.6 %collective-permute-start.13 = (bf16[3,384,384]{2,1,0:T(8,128)(2,1)}, bf16[3,384,384]{2,1,0:T(8,128)(2,1)}, u32[]{:S(2)}, u32[]{:S(2)}) collective-permute-start(bf16[3,384,384]{2,1,0:T(8,128)(2,1)} %squeeze.56), channel_id=1, source_target_pairs={{0,8},{8,16},{16,24},{1,9},{9,17},{17,25},{2,10},{10,18},{18,26},{... | collective-permute-start | bytes 2654216 | tf_op jit(solution)/shard_map/ppermute | solution.py:35
  517.9 17.8 %collective-permute-start.18 = (bf16[384,384]{1,0:T(8,128)(2,1)}, bf16[384,384]{1,0:T(8,128)(2,1)S(1)}, u32[]{:S(2)}, u32[]{:S(2)}) collective-permute-start(bf16[384,384]{1,0:T(8,128)(2,1)} %get-tuple-element.262), channel_id=1, source_target_pairs={{4,0},{5,1},{6,2},{7,3},{12,8},{13,9},{14,10},{15,11},{20,16},{21,... | collective-permute-start | bytes 884744 | tf_op jit(solution)/shard_map/ppermute | solution.py:35
  519.2 16.5 %collective-permute-start.19 = (bf16[384,384]{1,0:T(8,128)(2,1)S(1)}, bf16[384,384]{1,0:T(8,128)(2,1)}, u32[]{:S(2)}, u32[]{:S(2)}) collective-permute-start(bf16[384,384]{1,0:T(8,128)(2,1)S(1)} %get-tuple-element.263), channel_id=1, source_target_pairs={{0,4},{1,5},{2,6},{3,7},{8,12},{9,13},{10,14},{11,15},{16,20},{17,... | collective-permute-start | bytes 884744 | tf_op jit(solution)/shard_map/ppermute | solution.py:35
  528.2 9.5 %collective-permute-start.14 = (bf16[384,384]{1,0:T(8,128)(2,1)}, bf16[384,384]{1,0:T(8,128)(2,1)S(1)}, u32[]{:S(2)}, u32[]{:S(2)}) collective-permute-start(bf16[384,384]{1,0:T(8,128)(2,1)} %get-tuple-element.264), channel_id=1, source_target_pairs={{4,0},{5,1},{6,2},{7,3},{12,8},{13,9},{14,10},{15,11},{20,16},{21,... | collective-permute-start | bytes 884744 | tf_op jit(solution)/shard_map/ppermute | solution.py:35
  529.5 9.2 %collective-permute-start.15 = (bf16[384,384]{1,0:T(8,128)(2,1)S(1)}, bf16[384,384]{1,0:T(8,128)(2,1)}, u32[]{:S(2)}, u32[]{:S(2)}) collective-permute-start(bf16[384,384]{1,0:T(8,128)(2,1)S(1)} %get-tuple-element.265), channel_id=1, source_target_pairs={{0,4},{1,5},{2,6},{3,7},{8,12},{9,13},{10,14},{11,15},{16,20},{17,... | collective-permute-start | bytes 884744 | tf_op jit(solution)/shard_map/ppermute | solution.py:35
  (17 other events, 235.4 us)
Sparse Core Ops, SparseCore 0:
  118.1 32.2 reduce-scatter.3
  153.0 17.4 all-gather.6
  172.9 79.8 all-gather.8
  255.1 78.0 all-gather.4
  343.3 31.1 reduce-scatter.5
  378.3 17.4 all-gather.10
  400.6 72.8 reduce-scatter.7
where the time goes:
time: 557 us; the launch traced here: 549 us
  waiting for transfers between devices  274 us (49%)
  local copies, waits for them, and re-layouts  84.7 us (15%)
  matrix products  66.8 us (12%)
  starting transfers between devices  66.1 us (12%)
  other arithmetic  41.6 us (7%)
  between operations  15.4 us (3%)
    all_gather x1, waiting for transfers between devices, shards(): lax.all_gather(up_weight, ('ta', 'ha'), axis=0, tiled=True)  82.3 us
    all_gather x1, waiting for transfers between devices, shards(): lax.all_gather(down_weight, ('ta', 'ha'), axis=1, tiled=True)  74.3 us
    reduce_scatter x1, waiting for transfers between devices, shards(): lax.psum_scatter(attn_part, 'wa', scatter_dimension=0, tiled=True)  32.4 us
    reduce_scatter x1, waiting for transfers between devices, shards(): lax.psum_scatter(norm_part, 'wa', scatter_dimension=0, tiled=True)  31.3 us
    ppermute x6, starting transfers between devices, extended(): lax.ppermute(tail, axis, [(i, (i + 1) % count) for i in range(ends)])  30.7 us
    ppermute x8, starting transfers between devices, from_behind(): return lax.ppermute(array, axis, pairs)  27 us
    all_gather x1, waiting for transfers between devices, shards(): stream_grad = lax.all_gather(grad_share, 'wa', axis=0, tiled=True)  17.5 us
    all_gather x1, waiting for transfers between devices, shards(): hidden_in = lax.all_gather(hidden_share, 'wa', axis=0, tiled=True)  15.8 us
  transfers between devices with their start and end apart: 27, of which 12 were waited for; matrix products, arithmetic and copies ran while one was open for 24% of the time, Pallas kernels for 0%

commit v1 on v0

--- a/solution.py
+++ b/solution.py
@@ -1,8 +1,10 @@
+import functools
 import math
 import jax
 import jax.numpy as jnp
 from jax import lax
 from jax.sharding import PartitionSpec as P
+from jax.lax import axis_index, axis_size, ppermute
 
 HS = 128
 TILE = 384
@@ -10,6 +12,25 @@
 TANH_SCALE = 0.7978845608028654
 CUBIC_COEF = 0.044715
 NEG_FILL = -1e30
+
+
+def rest_the_tiles(base_x, array_axis):
+    parts_n = axis_size("wa")
+    x_next = sorted(((nth, (nth + 1) % parts_n) for nth in range(parts_n)))
+    small = base_x
+    buffers = [small]
+    w = 1
+    while w < parts_n:
+        small = ppermute(small, "wa", x_next)
+        buffers.insert(0, small)
+        w += 1
+    val = jnp.concatenate(buffers, axis=array_axis)
+    current_block = axis_index("wa")
+    next_value = current_block + 1
+    return jnp.roll(val, next_value * base_x.shape[array_axis], axis=array_axis)
+
+
+remake_values = functools.partial(rest_the_tiles, array_axis=0)
 
 
 def extended(cells, sides, width):
@@ -141,7 +162,7 @@
     )
     normed, inv_std = layer_norm(residual)
     hidden_share = (normed * norm_gain).astype(jnp.bfloat16)
-    hidden_in = lax.all_gather(hidden_share, "wa", axis=0, tiled=True)
+    hidden_in = remake_values(hidden_share)
     up_full, down_full = (
         lax.all_gather(up_weight, ("ta", "ha"), axis=0, tiled=True),
         lax.all_gather(down_weight, ("ta", "ha"), axis=1, tiled=True),

time: 557 us -> 505 us (0.907)
  waiting for transfers between devices: 274 us -> 215 us
    all_gather x1, waiting for transfers between devices: 82.3 us -> 22.4 us  [shards(): lax.all_gather(up_weight, ('ta', 'ha'), axis=0, tiled=True)]
    ppermute x0 -> x3, waiting for transfers between devices: none -> 18.4 us  [rest_the_tiles(): small = ppermute(small, 'wa', x_next)]
    all_gather x1 -> x0, waiting for transfers between devices: 15.8 us -> none  [shards(): hidden_in = lax.all_gather(hidden_share, 'wa', axis=0, tiled=True)]
    unnamed x26 -> x32, local copies, waits for them, and re-layouts: 12.3 us -> 16.6 us
  transfers between devices with their start and end apart: 27 -> 29, of which waited for: 12 -> 14; matrix products, arithmetic and copies ran while one was open for 24% -> 28% of each run, Pallas kernels for 0% -> 0%
where the time goes in v1:
time: 505 us; the launch traced here: 497 us
  waiting for transfers between devices  215 us (43%)
  local copies, waits for them, and re-layouts  89.1 us (18%)
  matrix products  66.7 us (13%)
  starting transfers between devices  66.1 us (13%)
  other arithmetic  42.7 us (8%)
  between operations  16.8 us (3%)
    all_gather x1, waiting for transfers between devices, shards(): lax.all_gather(down_weight, ('ta', 'ha'), axis=1, tiled=True)  74 us
    reduce_scatter x1, waiting for transfers between devices, shards(): lax.psum_scatter(norm_part, 'wa', scatter_dimension=0, tiled=True)  31.4 us
    reduce_scatter x1, waiting for transfers between devices, shards(): lax.psum_scatter(attn_part, 'wa', scatter_dimension=0, tiled=True)  31.3 us
    ppermute x6, starting transfers between devices, extended(): lax.ppermute(tail, axis, [(i, (i + 1) % count) for i in range(ends)])  30.7 us
    ppermute x8, starting transfers between devices, from_behind(): return lax.ppermute(array, axis, pairs)  27 us
    all_gather x1, waiting for transfers between devices, shards(): lax.all_gather(up_weight, ('ta', 'ha'), axis=0, tiled=True)  22.4 us
    ppermute x3, waiting for transfers between devices, rest_the_tiles(): small = ppermute(small, 'wa', x_next)  18.4 us
    all_gather x1, waiting for transfers between devices, shards(): stream_grad = lax.all_gather(grad_share, 'wa', axis=0, tiled=True)  17.6 us
  transfers between devices with their start and end apart: 29, of which 14 were waited for; matrix products, arithmetic and copies ran while one was open for 28% of the time, Pallas kernels for 0%

profile of v1, /device:TPU:0, one launch (start us, length us, event | category | flops | bytes accessed | tf_op | source)
XLA Modules:
  0.0 496.8 jit_solution(10577667394080214062)
XLA Ops:
  31.5 6.4 %collective-permute-start.6 = (bf16[3,1,384,384]{3,2,1,0:T(8,128)(2,1)S(1)}, bf16[3,1,384,384]{3,2,1,0:T(8,128)(2,1)}, u32[]{:S(2)}, u32[]{:S(2)}) collective-permute-start(bf16[3,1,384,384]{3,2,1,0:T(8,128)(2,1)S(1)} %constant_dynamic-update-slice_fusion.1), channel_id=1, source_target_pairs={{0,4},{1,5},{2,6},{3,7},{8,12},{9,13},{10,14},{11,15},{16,20},{17,... | collective-permute-start | bytes 2654216 | tf_op jit(solution)/shard_map/ppermute | solution.py:44
  57.4 6.5 %collective-permute-done.2 = bf16[3,1,1]{0,2,1:T(2,128)(2,1)S(1)} collective-permute-done((bf16[3,1,1]{0,2,1:T(2,128)(2,1)S(1)}, bf16[3,1,1]{0,2,1:T(2,128)(2,1)S(1)}, u32[]{:S(2)}, u32[]{:S(2)}) %collective-permute-start.2) | collective-permute-done | bytes 38 | tf_op jit(solution)/shard_map/ppermute | solution.py:44
  72.9 7.7 %reshape.147 = bf16[3456,3,128]{2,1,0:T(4,128)(2,1)} reshape(bf16[3,3,384,384]{3,2,1,0:T(8,128)(2,1)} %pad_maximum_fusion.1) | data formatting | bytes 5308416 | tf_op jit(solution)/shard_map/while/body/eval_jaxpr/reshape | solution.py:124
  87.8 7.7 %reshape.146 = bf16[3456,3,128]{2,1,0:T(4,128)(2,1)} reshape(bf16[3,3,384,384]{3,2,1,0:T(8,128)(2,1)} %pad_maximum_fusion) | data formatting | bytes 5308416 | tf_op jit(solution)/shard_map/while/body/eval_jaxpr/reshape | solution.py:123
  99.5 16.9 %while.44 = (s32[]{:T(128)}, f32[3,384,128]{1,2,0:T(8,128)S(1)}, bf16[3,384,128]{2,1,0:T(8,128)(2,1)S(1)}, bf16[3,3456,128]{2,1,0:T(8,128)(2,1)}, bf16[3,3456,128]{2,1,0:T(8,128)(2,1)}, /*index=5*/f32[9]{0:T(128)S(1)}, s32[]{:T(128)}) while((s32[]{:T(128)}, f32[3,384,128]{1,2,0:T(8,128)S(1)}, bf16[3,384,128]{2,1,0:T(8,128)(2,1)S(1)}, ...), condition=%wide.region_3.4_spmd.clone, body=%wide.region_0.3_spmd.clone.sunk | while | flops 690093312 | bytes 18014980 | solution.py:147
  119.9 31.3 %reduce-scatter.4.cloned.1.call-done = f32[96,1536]{1,0:T(8,128)} async-done(((f32[384,1536]{1,0:T(8,128)}), f32[96,1536]{1,0:T(8,128)}) %reduce-scatter.4.cloned.1.call-update) | async-done | bytes 589840 | tf_op jit(solution)/shard_map/reduce_scatter | solution.py:154
  153.0 6.1 %collective-permute-done.12 = bf16[96,1536]{1,0:T(8,128)(2,1)S(1)} collective-permute-done((bf16[96,1536]{1,0:T(8,128)(2,1)S(1)}, bf16[96,1536]{1,0:T(8,128)(2,1)S(1)}, u32[]{:S(2)}, u32[]{:S(2)}) %collective-permute-start.12) | collective-permute-done | bytes 294944 | tf_op jit(solution)/shard_map/ppermute | solution.py:24
  159.2 6.1 %collective-permute-done.13 = bf16[96,1536]{1,0:T(8,128)(2,1)S(1)} collective-permute-done((bf16[96,1536]{1,0:T(8,128)(2,1)S(1)}, bf16[96,1536]{1,0:T(8,128)(2,1)S(1)}, u32[]{:S(2)}, u32[]{:S(2)}) %collective-permute-start.13) | collective-permute-done | bytes 294944 | tf_op jit(solution)/shard_map/ppermute | solution.py:24
  165.8 6.1 %collective-permute-done.14 = bf16[96,1536]{1,0:T(8,128)(2,1)S(1)} collective-permute-done((bf16[96,1536]{1,0:T(8,128)(2,1)S(1)}, bf16[96,1536]{1,0:T(8,128)(2,1)S(1)}, u32[]{:S(2)}, u32[]{:S(2)}) %collective-permute-start.14) | collective-permute-done | bytes 294944 | tf_op jit(solution)/shard_map/ppermute | solution.py:24
  178.0 22.4 %all-gather.6.cloned.1.call-done = bf16[1536,1536]{1,0:T(8,128)(2,1)} async-done(((bf16[192,1536]{1,0:T(8,128)(2,1)}), bf16[1536,1536]{1,0:T(8,128)(2,1)}) %all-gather.6.cloned.1.call-update) | async-done | bytes 4718608 | tf_op jit(solution)/shard_map/all_gather | solution.py:167
  200.4 6.1 %fusion.54 = f32[384,1536]{1,0:T(8,128)} fusion(bf16[1536,1536]{1,0:T(8,128)(2,1)} %all-gather.6.cloned.1.call-done, bf16[768,1536]{1,0:T(8,128)(2,1)} %constant_dynamic-update-slice_fusion.7, s32[]{:T(128)S(6)} %select_n.28), kind=kOutput, calls=%fused_computation.72 | convolution fusion | flops 1811939328 | bytes 8257540 | tf_op jit(solution)/shard_map/dot_general | solution.py:170
  206.4 74.0 %all-gather.4.cloned.1.call-done = bf16[1536,1536]{0,1:T(8,128)(2,1)} async-done(((bf16[1536,192]{0,1:T(8,128)(2,1)}), bf16[1536,1536]{0,1:T(8,128)(2,1)}) %all-gather.4.cloned.1.call-update) | async-done | bytes 4718608 | tf_op jit(solution)/shard_map/all_gather | solution.py:168
  280.4 10.0 %fusion.58 = f32[384,1536]{1,0:T(8,128)} fusion(bf16[1536,1536]{1,0:T(8,128)(2,1)} %all-gather.6.cloned.1.call-done, bf16[1536,1536]{0,1:T(8,128)(2,1)} %all-gather.4.cloned.1.call-done, f32[384,1536]{1,0:T(8,128)} %fusion.54, bf16[1,1,384,1536]{3,2,1,0:T(8,128)(2,1)} %param.23), kind=kOutput, calls=%fused_computation.77 | convolution fusion | flops 3635085312 | bytes 15335424 | tf_op jit(solution)/shard_map/tf,df->td/dot_general | solution.py:173
  290.5 31.4 %reduce-scatter.6.cloned.1.call-done = f32[96,1536]{1,0:T(8,128)} async-done(((f32[384,1536]{1,0:T(8,128)}), f32[96,1536]{1,0:T(8,128)}) %reduce-scatter.6.cloned.1.call-update) | async-done | bytes 589840 | tf_op jit(solution)/shard_map/reduce_scatter | solution.py:174
  325.6 17.6 %all-gather.8.cloned.1.call-done = bf16[384,1536]{1,0:T(8,128)(2,1)} async-done(((bf16[96,1536]{1,0:T(8,128)(2,1)}), bf16[384,1536]{1,0:T(8,128)(2,1)}) %all-gather.8.cloned.1.call-update) | async-done | bytes 1179664 | tf_op jit(solution)/shard_map/all_gather | solution.py:179
  347.9 43.7 %while.45 = (s32[]{:T(128)}, bf16[3,384,128]{1,2,0:T(8,128)(2,1)S(1)}, bf16[3,3456,128]{2,1,0:T(8,128)(2,1)}, bf16[3,3456,128]{2,1,0:T(8,128)(2,1)}, bf16[3,384,...) while((s32[]{:T(128)}, ...), condition=%wide.region_14.15_spmd.clone, body=%wide.region_10.14_spmd.clone.sunk | while | flops 1723513728 | bytes 71701848 | solution.py:218
  394.5 5.5 %copy.58 = bf16[1152,3,128]{2,1,0:T(4,128)(2,1)S(1)} copy(bf16[1152,3,128]{2,0,1:T(8,128)(2,1)S(1)} %get-tuple-element.256) | data formatting | bytes 1769472 | tf_op jit(solution)/shard_map/slice | solution.py:247
  403.4 5.6 %copy.59 = bf16[1152,3,128]{2,1,0:T(4,128)(2,1)S(1)} copy(bf16[1152,3,128]{2,0,1:T(8,128)(2,1)} %get-tuple-element.257) | data formatting | bytes 1769472 | tf_op jit(solution)/shard_map/slice | solution.py:247
  411.0 5.5 %collective-permute-start.20 = (bf16[3,384,384]{2,1,0:T(8,128)(2,1)}, bf16[3,384,384]{2,1,0:T(8,128)(2,1)}, u32[]{:S(2)}, u32[]{:S(2)}) collective-permute-start(bf16[3,384,384]{2,1,0:T(8,128)(2,1)} %squeeze.59), channel_id=1, source_target_pairs={{0,8},{8,16},{16,24},{1,9},{9,17},{17,25},{2,10},{10,18},{18,26},{... | collective-permute-start | bytes 2654216 | tf_op jit(solution)/shard_map/ppermute | solution.py:56
  419.9 5.5 %copy.55 = bf16[1152,3,128]{2,1,0:T(4,128)(2,1)S(1)} copy(bf16[1152,3,128]{2,0,1:T(8,128)(2,1)S(1)} %get-tuple-element.259) | data formatting | bytes 1769472 | tf_op jit(solution)/shard_map/slice | solution.py:247
  428.7 5.6 %copy.56 = bf16[1152,3,128]{2,1,0:T(4,128)(2,1)S(1)} copy(bf16[1152,3,128]{2,0,1:T(8,128)(2,1)} %get-tuple-element.260) | data formatting | bytes 1769472 | tf_op jit(solution)/shard_map/slice | solution.py:247
  436.3 5.7 %collective-permute-start.16 = (bf16[3,384,384]{2,1,0:T(8,128)(2,1)}, bf16[3,384,384]{2,1,0:T(8,128)(2,1)}, u32[]{:S(2)}, u32[]{:S(2)}) collective-permute-start(bf16[3,384,384]{2,1,0:T(8,128)(2,1)} %squeeze.56), channel_id=1, source_target_pairs={{0,8},{8,16},{16,24},{1,9},{9,17},{17,25},{2,10},{10,18},{18,26},{... | collective-permute-start | bytes 2654216 | tf_op jit(solution)/shard_map/ppermute | solution.py:56
  441.9 5.9 %copy.57 = f32[1152,3,128]{2,1,0:T(4,128)} copy(f32[1152,3,128]{2,0,1:T(8,128)S(1)} %get-tuple-element.258) | data formatting | bytes 3538944 | tf_op jit(solution)/shard_map/convert_element_type | solution.py:244
  452.1 5.9 %copy.54 = f32[1152,3,128]{2,1,0:T(4,128)} copy(f32[1152,3,128]{2,0,1:T(8,128)S(1)} %copy-done.2) | data formatting | bytes 3538944 | tf_op jit(solution)/shard_map/convert_element_type | solution.py:243
  (193 shorter events, 195.0 us)
Async XLA Ops:
  8.0 143.2 %reduce-scatter.4.cloned.1.call-start = ((), (), s32[]{:S(2)}) async-start(), calls=%async_computation.4 | async-start | bytes 2949120 | tf_op jit(solution)/shard_map/reduce_scatter | solution.py:154
  8.1 12.6 %collective-permute-start.8 = (bf16[1,1,384,384]{3,2,1,0:T(8,128)(2,1)}, bf16[1,1,384,384]{3,2,1,0:T(8,128)(2,1)S(1)}, u32[]{:S(2)}, u32[]{:S(2)}) collective-permute-start(bf16[1,1,384,384]{3,2,1,0:T(8,128)(2,1)} %param.17), channel_id=1, source_target_pairs={{0,8},{8,16},{16,24},{1,9},{9,17},{17,25},{2,10},{10,18},{18,26},{... | collective-permute-start | bytes 884744 | tf_op jit(solution)/shard_map/ppermute | solution.py:44
  13.2 11.5 %collective-permute-start.9 = (bf16[1,1,384,384]{3,2,1,0:T(8,128)(2,1)}, bf16[1,1,384,384]{3,2,1,0:T(8,128)(2,1)S(1)}, u32[]{:S(2)}, u32[]{:S(2)}) collective-permute-start(bf16[1,1,384,384]{3,2,1,0:T(8,128)(2,1)} %param.17), channel_id=1, source_target_pairs={{8,0},{16,8},{24,16},{9,1},{17,9},{25,17},{10,2},{18,10},{26,18},{... | collective-permute-start | bytes 884744 | tf_op jit(solution)/shard_map/ppermute | solution.py:46
  14.5 15.9 %collective-permute-start.4 = (bf16[1,1,384,384]{3,2,1,0:T(8,128)(2,1)}, bf16[1,1,384,384]{3,2,1,0:T(8,128)(2,1)S(1)}, u32[]{:S(2)}, u32[]{:S(2)}) collective-permute-start(bf16[1,1,384,384]{3,2,1,0:T(8,128)(2,1)} %param.16), channel_id=1, source_target_pairs={{0,8},{8,16},{16,24},{1,9},{9,17},{17,25},{2,10},{10,18},{18,26},{... | collective-permute-start | bytes 884744 | tf_op jit(solution)/shard_map/ppermute | solution.py:44
  19.0 12.4 %collective-permute-start.5 = (bf16[1,1,384,384]{3,2,1,0:T(8,128)(2,1)}, bf16[1,1,384,384]{3,2,1,0:T(8,128)(2,1)S(1)}, u32[]{:S(2)}, u32[]{:S(2)}) collective-permute-start(bf16[1,1,384,384]{3,2,1,0:T(8,128)(2,1)} %param.16), channel_id=1, source_target_pairs={{8,0},{16,8},{24,16},{9,1},{17,9},{25,17},{10,2},{18,10},{26,18},{... | collective-permute-start | bytes 884744 | tf_op jit(solution)/shard_map/ppermute | solution.py:46
  24.7 44.9 %collective-permute-start.10 = (bf16[3,1,384,384]{3,2,1,0:T(8,128)(2,1)S(1)}, bf16[3,1,384,384]{3,2,1,0:T(8,128)(2,1)}, u32[]{:S(2)}, u32[]{:S(2)}) collective-permute-start(bf16[3,1,384,384]{3,2,1,0:T(8,128)(2,1)S(1)} %constant_dynamic-update-slice_fusion.4), channel_id=1, source_target_pairs={{0,4},{1,5},{2,6},{3,7},{8,12},{9,13},{10,14},{11,15},{16,20},{17,... | collective-permute-start | bytes 2654216 | tf_op jit(solution)/shard_map/ppermute | solution.py:44
  29.1 40.5 %collective-permute-start.11 = (bf16[3,1,384,384]{3,2,1,0:T(8,128)(2,1)S(1)}, bf16[3,1,384,384]{3,2,1,0:T(8,128)(2,1)}, u32[]{:S(2)}, u32[]{:S(2)}) collective-permute-start(bf16[3,1,384,384]{3,2,1,0:T(8,128)(2,1)S(1)} %constant_dynamic-update-slice_fusion.4), channel_id=1, source_target_pairs={{4,0},{5,1},{6,2},{7,3},{12,8},{13,9},{14,10},{15,11},{20,16},{21,... | collective-permute-start | bytes 2654216 | tf_op jit(solution)/shard_map/ppermute | solution.py:46
  31.5 53.0 %collective-permute-start.6 = (bf16[3,1,384,384]{3,2,1,0:T(8,128)(2,1)S(1)}, bf16[3,1,384,384]{3,2,1,0:T(8,128)(2,1)}, u32[]{:S(2)}, u32[]{:S(2)}) collective-permute-start(bf16[3,1,384,384]{3,2,1,0:T(8,128)(2,1)S(1)} %constant_dynamic-update-slice_fusion.1), channel_id=1, source_target_pairs={{0,4},{1,5},{2,6},{3,7},{8,12},{9,13},{10,14},{11,15},{16,20},{17,... | collective-permute-start | bytes 2654216 | tf_op jit(solution)/shard_map/ppermute | solution.py:44
  37.9 46.6 %collective-permute-start.7 = (bf16[3,1,384,384]{3,2,1,0:T(8,128)(2,1)S(1)}, bf16[3,1,384,384]{3,2,1,0:T(8,128)(2,1)}, u32[]{:S(2)}, u32[]{:S(2)}) collective-permute-start(bf16[3,1,384,384]{3,2,1,0:T(8,128)(2,1)S(1)} %constant_dynamic-update-slice_fusion.1), channel_id=1, source_target_pairs={{4,0},{5,1},{6,2},{7,3},{12,8},{13,9},{14,10},{15,11},{20,16},{21,... | collective-permute-start | bytes 2654216 | tf_op jit(solution)/shard_map/ppermute | solution.py:46
  51.9 12.1 %collective-permute-start.2 = (bf16[3,1,1]{0,2,1:T(2,128)(2,1)S(1)}, bf16[3,1,1]{0,2,1:T(2,128)(2,1)S(1)}, u32[]{:S(2)}, u32[]{:S(2)}) collective-permute-start(bf16[3,1,1]{0,2,1:T(2,128)(2,1)S(1)} %pad_maximum_fusion.2), channel_id=1, source_target_pairs={{0,4},{1,5},{2,6},{3,7},{8,12},{9,13},{10,14},{11,15},{16,20},{17,... | collective-permute-start | bytes 26 | tf_op jit(solution)/shard_map/ppermute | solution.py:44
  118.7 81.7 %all-gather.6.cloned.1.call-start = ((), (), s32[]{:S(2)}) async-start(), calls=%async_computation.5 | async-start | bytes 5308416 | tf_op jit(solution)/shard_map/all_gather | solution.py:167
  119.3 161.1 %all-gather.4.cloned.1.call-start = ((), (), s32[]{:S(2)}) async-start(), calls=%async_computation.3 | async-start | bytes 5308416 | tf_op jit(solution)/shard_map/all_gather | solution.py:168
  119.9 202.1 %reduce-scatter.6.cloned.1.call-start = ((), (), s32[]{:S(2)}) async-start(), calls=%async_computation.6 | async-start | bytes 2949120 | tf_op jit(solution)/shard_map/reduce_scatter | solution.py:174
  165.3 6.6 %collective-permute-start.14 = (bf16[96,1536]{1,0:T(8,128)(2,1)S(1)}, bf16[96,1536]{1,0:T(8,128)(2,1)S(1)}, u32[]{:S(2)}, u32[]{:S(2)}) collective-permute-start(bf16[96,1536]{1,0:T(8,128)(2,1)S(1)} %collective-permute-done.13), channel_id=1, source_target_pairs={{0,1},{1,2},{2,3},{3,0},{4,5},{5,6},{6,7},{7,4},{8,9},{9,10},{10,1... | collective-permute-start | bytes 884744 | tf_op jit(solution)/shard_map/ppermute | solution.py:24
  290.5 52.7 %all-gather.8.cloned.1.call-start = ((), (), s32[]{:S(2)}) async-start(), calls=%async_computation.7 | async-start | bytes 1474560 | tf_op jit(solution)/shard_map/all_gather | solution.py:179
  325.5 162.6 %reduce-scatter.8.cloned.1.call-start = ((), (), s32[]{:S(2)}) async-start(), calls=%async_computation.8 | async-start | bytes 2654208 | tf_op jit(solution)/shard_map/reduce_scatter | solution.py:183
  402.0 59.0 %collective-permute-start.19 = (bf16[3,384,384]{2,1,0:T(8,128)(2,1)}, bf16[3,384,384]{2,1,0:T(8,128)(2,1)}, u32[]{:S(2)}, u32[]{:S(2)}) collective-permute-start(bf16[3,384,384]{2,1,0:T(8,128)(2,1)} %squeeze.58), channel_id=1, source_target_pairs={{8,0},{16,8},{24,16},{9,1},{17,9},{25,17},{10,2},{18,10},{26,18},{... | collective-permute-start | bytes 2654216 | tf_op jit(solution)/shard_map/ppermute | solution.py:56
  411.0 50.0 %collective-permute-start.20 = (bf16[3,384,384]{2,1,0:T(8,128)(2,1)}, bf16[3,384,384]{2,1,0:T(8,128)(2,1)}, u32[]{:S(2)}, u32[]{:S(2)}) collective-permute-start(bf16[3,384,384]{2,1,0:T(8,128)(2,1)} %squeeze.59), channel_id=1, source_target_pairs={{0,8},{8,16},{16,24},{1,9},{9,17},{17,25},{2,10},{10,18},{18,26},{... | collective-permute-start | bytes 2654216 | tf_op jit(solution)/shard_map/ppermute | solution.py:56
  427.4 44.5 %collective-permute-start.15 = (bf16[3,384,384]{2,1,0:T(8,128)(2,1)}, bf16[3,384,384]{2,1,0:T(8,128)(2,1)}, u32[]{:S(2)}, u32[]{:S(2)}) collective-permute-start(bf16[3,384,384]{2,1,0:T(8,128)(2,1)} %squeeze.55), channel_id=1, source_target_pairs={{8,0},{16,8},{24,16},{9,1},{17,9},{25,17},{10,2},{18,10},{26,18},{... | collective-permute-start | bytes 2654216 | tf_op jit(solution)/shard_map/ppermute | solution.py:56
  436.3 35.6 %collective-permute-start.16 = (bf16[3,384,384]{2,1,0:T(8,128)(2,1)}, bf16[3,384,384]{2,1,0:T(8,128)(2,1)}, u32[]{:S(2)}, u32[]{:S(2)}) collective-permute-start(bf16[3,384,384]{2,1,0:T(8,128)(2,1)} %squeeze.56), channel_id=1, source_target_pairs={{0,8},{8,16},{16,24},{1,9},{9,17},{17,25},{2,10},{10,18},{18,26},{... | collective-permute-start | bytes 2654216 | tf_op jit(solution)/shard_map/ppermute | solution.py:56
  465.3 17.8 %collective-permute-start.21 = (bf16[384,384]{1,0:T(8,128)(2,1)}, bf16[384,384]{1,0:T(8,128)(2,1)S(1)}, u32[]{:S(2)}, u32[]{:S(2)}) collective-permute-start(bf16[384,384]{1,0:T(8,128)(2,1)} %get-tuple-element.262), channel_id=1, source_target_pairs={{4,0},{5,1},{6,2},{7,3},{12,8},{13,9},{14,10},{15,11},{20,16},{21,... | collective-permute-start | bytes 884744 | tf_op jit(solution)/shard_map/ppermute | solution.py:56
  466.6 16.5 %collective-permute-start.22 = (bf16[384,384]{1,0:T(8,128)(2,1)S(1)}, bf16[384,384]{1,0:T(8,128)(2,1)}, u32[]{:S(2)}, u32[]{:S(2)}) collective-permute-start(bf16[384,384]{1,0:T(8,128)(2,1)S(1)} %get-tuple-element.263), channel_id=1, source_target_pairs={{0,4},{1,5},{2,6},{3,7},{8,12},{9,13},{10,14},{11,15},{16,20},{17,... | collective-permute-start | bytes 884744 | tf_op jit(solution)/shard_map/ppermute | solution.py:56
  475.6 9.6 %collective-permute-start.17 = (bf16[384,384]{1,0:T(8,128)(2,1)}, bf16[384,384]{1,0:T(8,128)(2,1)S(1)}, u32[]{:S(2)}, u32[]{:S(2)}) collective-permute-start(bf16[384,384]{1,0:T(8,128)(2,1)} %get-tuple-element.264), channel_id=1, source_target_pairs={{4,0},{5,1},{6,2},{7,3},{12,8},{13,9},{14,10},{15,11},{20,16},{21,... | collective-permute-start | bytes 884744 | tf_op jit(solution)/shard_map/ppermute | solution.py:56
  476.9 9.3 %collective-permute-start.18 = (bf16[384,384]{1,0:T(8,128)(2,1)S(1)}, bf16[384,384]{1,0:T(8,128)(2,1)}, u32[]{:S(2)}, u32[]{:S(2)}) collective-permute-start(bf16[384,384]{1,0:T(8,128)(2,1)S(1)} %get-tuple-element.265), channel_id=1, source_target_pairs={{0,4},{1,5},{2,6},{3,7},{8,12},{9,13},{10,14},{11,15},{16,20},{17,... | collective-permute-start | bytes 884744 | tf_op jit(solution)/shard_map/ppermute | solution.py:56
  (19 other events, 247.9 us)
Sparse Core Ops, SparseCore 0:
  118.8 32.3 reduce-scatter.3
  290.6 31.2 reduce-scatter.5
  325.6 17.4 all-gather.7
Sparse Core Ops, SparseCore 1:
  121.6 78.7 all-gather.5
  202.7 77.7 all-gather.3
  348.0 72.7 reduce-scatter.7
